TPU v7x, 128 devices: a whole 4x4x4 slice. The times are simulated.
128 devices in a mesh: wide: 16 (over x, z), narrow: 8 (over y, core).
Axes of the slice: x: 4, y: 4, z: 4, core: 2. Of those that a mesh axis runs over, the one named last changes fastest.
Arguments:
- activations: bfloat16 [4096, 16384], P('wide', 'narrow'), may hold values from -6 to 6
- grad_out: bfloat16 [4096, 8192], P('narrow', 'wide'), may hold values from -0.09375 to 0.09375
- momentum: float32 [8192, 16384], P('wide', 'narrow'), may hold values from -90 to 90
- right_factor: float32 [16384, 512], P('narrow'), may hold values from -0.046875 to 0.046875
Outputs:
- new_momentum: float32 [8192, 16384], P('wide', 'narrow')
- new_right: float32 [16384, 512], P('narrow')
- update: bfloat16 [8192, 16384], P('wide', 'narrow')
All inputs are finite; a program needn't handle non-finite values.
Results may differ from a plain program's by a relative error of at most 0.0012.
Values may be sent and summed in bfloat16 or wider, within the bound.
A program may use at most 128 MiB of HBM per device.

v0:
```python
import math
import jax
import jax.numpy as jnp
from jax import lax
from jax.sharding import Mesh
from jax.sharding import PartitionSpec as P

DOUT = 8192
DIN = 16384
RANK = 512
NARROW = ("narrow_0", "narrow_1")
WIDE = ("wide_0", "wide_1")
FEEDBACK = 0.05
EPSILON = 1e-06


def sent_to_all(array, axis):
    devices = lax.axis_size(axis)
    return lax.all_to_all(
        jnp.broadcast_to(array[None], (devices, *array.shape)), axis, 0, 0, tiled=True
    )


def laid_out(tiles, dim):
    tiles = jnp.moveaxis(tiles, 0, dim)
    lengths = tiles.shape
    return tiles.reshape(*lengths[:dim], lengths[dim] * lengths[dim + 1], *lengths[dim + 2 :])


def gathered_by_axis(array, axes, dim):
    far, near = axes
    tiles = sent_to_all(sent_to_all(array, far), near)
    return laid_out(tiles.swapaxes(0, 1).reshape(-1, *array.shape), dim)


def split_up(array, dim, devices):
    before, after = (array.shape[:dim], array.shape[dim + 1 :])
    return jnp.moveaxis(array.reshape(*before, devices, -1, *after), dim, 0)


def summed_on_arrival(array, axis, dim):
    tiles = split_up(array, dim, lax.axis_size(axis))
    arrived = lax.all_to_all(tiles, axis, split_axis=0, concat_axis=0, tiled=True)
    return arrived.sum(axis=0)


def padded_to(lines, devices):
    spare = -len(lines) % devices
    return jnp.pad(lines, [(0, spare)] + [(0, 0)] * (lines.ndim - 1))


def summed_rows(array, axes, dim):
    far, near = axes
    own = summed_on_arrival(split_up(array, dim, lax.axis_size(far)), near, dim + 1)
    return jnp.sum(lax.all_to_all(own, far, 0, 0, tiled=True), axis=0)


def total_of(array, axes):
    lines = array.reshape(-1, array.shape[-1])
    padded = padded_to(lines, lax.axis_size(axes[0]) * lax.axis_size(axes[1]))
    whole = gathered_by_axis(summed_rows(padded, axes, 0), axes, 0)
    return lax.slice_in_dim(whole, 0, len(lines)).reshape(array.shape)


def gathered_copies(array, axis, dim):
    return laid_out(sent_to_all(array, axis), dim)


def own_rows(total, axes):
    for axis in axes:
        total = lax.psum_scatter(total, axis, scatter_dimension=0, tiled=True)
    return total


def taken_together(array, axis):
    return sent_to_all(array, axis).sum(axis=0)


def over_axes(array, axes):
    far, near = axes
    nearer = taken_together(array, near)
    return taken_together(nearer, far)


def body(activations, grad_out, momentum, right_factor):
    highest = lax.Precision.HIGHEST
    out_rows = gathered_by_axis(grad_out, ("narrow_0", "narrow_1"), 0)
    gradient = lax.dot_general(
        out_rows,
        lax.all_gather(activations, WIDE, axis=0, tiled=True),
        (((0,), (0,)), ((), ())),
        preferred_element_type=jnp.float32,
    )
    buffer = momentum + gradient
    left_share = summed_on_arrival(
        jnp.dot(buffer, right_factor, precision=highest, preferred_element_type=jnp.float32),
        NARROW,
        0,
    )
    gram_local = jnp.dot(
        left_share.T, left_share, precision=highest, preferred_element_type=jnp.float32
    )
    gram_matrix = total_of(gram_local, (("wide_0", "wide_1", "narrow_0"), "narrow_1"))
    lower_factor = jnp.linalg.cholesky(gram_matrix)
    ortho_share = jax.scipy.linalg.solve_triangular(lower_factor, left_share.T, lower=True).T
    ortho_left = gathered_copies(ortho_share, NARROW, 0)
    right_share = own_rows(
        lax.dot_general(
            buffer,
            ortho_left,
            (((0,), (0,)), ((), ())),
            precision=highest,
            preferred_element_type=jnp.float32,
        ),
        WIDE,
    )
    col_squares = over_axes(
        jnp.sum(right_share * right_share, axis=0), (("wide_0", "wide_1", "narrow_0"), "narrow_1")
    )
    right_raw = lax.all_gather(right_share, WIDE, axis=0, tiled=True)
    feedback = lax.dot_general(
        ortho_left,
        right_raw,
        (((1,), (1,)), ((), ())),
        precision=highest,
        preferred_element_type=jnp.float32,
    )
    new_momentum = buffer - FEEDBACK * feedback
    new_right = right_raw / (jnp.sqrt(col_squares) + EPSILON)
    update_scale = math.sqrt(DOUT * DIN / RANK)
    product = lax.dot_general(
        ortho_left,
        new_right,
        (((1,), (1,)), ((), ())),
        precision=highest,
        preferred_element_type=jnp.float32,
    )
    update = (update_scale * product).astype(jnp.bfloat16)
    return (new_momentum, new_right, update)


def solution(mesh):
    finer = Mesh(mesh.devices.reshape(4, 4, 4, 2), ("wide_0", "wide_1", "narrow_0", "narrow_1"))
    in_specs = (P(WIDE, NARROW), P(NARROW, WIDE), P(WIDE, NARROW), P(NARROW, None))
    out_specs = (P(WIDE, NARROW), P(NARROW, None), P(WIDE, NARROW))
    return jax.shard_map(body, mesh=finer, in_specs=in_specs, out_specs=out_specs, check_vma=False)
```

profile of v0, /device:TPU:1, one launch (start us, length us, event | category | flops | bytes accessed | tf_op | source)
XLA Modules:
  0.0 525.0 jit_solution(6163401556393695659)
XLA Ops:
  9.1 30.2 %all_to_all.52 = bf16[4,512,512]{2,1,0:T(8,128)(2,1)S(1)} all-to-all(bf16[4,512,512]{2,1,0:T(8,128)(2,1)S(1)} %broadcast_in_dim.15), channel_id=1, replica_groups=mesh['wide_0'=4,'wide_1'=4,'narrow_0'=4,'narrow_1'=2] {'narrow_0'}, dimensions={0} | all-to-all | bytes 4194304 | tf_op jit(solution)/shard_map/all_to_all | solution.py:19
  39.7 8.6 %all_to_all.53 = bf16[2,4,512,512]{3,2,1,0:T(8,128)(2,1)S(1)} all-to-all(bf16[2,4,512,512]{3,2,1,0:T(8,128)(2,1)S(1)} %broadcast_in_dim.16), channel_id=1, replica_groups=mesh['wide_0'=4,'wide_1'=4,'narrow_0'=4,'narrow_1'=2] {'narrow_1'}, dimensions={0} | all-to-all | bytes 8388608 | tf_op jit(solution)/shard_map/all_to_all | solution.py:19
  48.3 2.5 copy.28
  50.8 74.0 %all-gather.3.cloned.1.call-done = bf16[4096,2048]{1,0:T(8,128)(2,1)} async-done(((bf16[256,2048]{1,0:T(8,128)(2,1)}), bf16[4096,2048]{1,0:T(8,128)(2,1)}) %all-gather.3.cloned.1.call-update) | async-done | bytes 16777232 | tf_op jit(solution)/shard_map/all_gather | solution.py:90
  124.8 14.4 %convolution_add_fusion = f32[512,2048]{1,0:T(8,128)S(1)} fusion(f32[512,2048]{1,0:T(8,128)} %param.6, bf16[4096,512]{1,0:T(8,128)(2,1)} %bitcast.79, bf16[4096,2048]{1,0:T(8,128)(2,1)} %all-gather.3.cloned.1.call-done), kind=kOutput, calls=%fused_computation.4 | convolution fusion | flops 8590983168 | bytes 29360128 | tf_op jit(solution)/shard_map/dot_general | solution.py:88
  139.2 6.9 %fusion.33 = f32[512,512]{1,0:T(8,128)S(1)} fusion(f32[512,2048]{1,0:T(8,128)S(1)} %convolution_add_fusion, f32[2048,512]{1,0:T(8,128)S(1)} %copy-done.4), kind=kOutput, calls=%fused_computation.76 | convolution fusion | flops 6442450944 | bytes 9437184 | tf_op jit(solution)/shard_map/dot_general | solution.py:96
  146.1 19.9 %all_to_all.54 = f32[8,64,512]{2,1,0:T(8,128)S(1)} all-to-all(f32[8,64,512]{2,1,0:T(8,128)S(1)} %bitcast.78), channel_id=1, replica_groups=mesh['wide_0'=4,'wide_1'=4,'narrow_0'=4,'narrow_1'=2] {'narrow_0','narro..., dimensions={0} | all-to-all | bytes 2097152 | tf_op jit(solution)/shard_map/all_to_all | solution.py:43
  167.2 5.2 all_to_all.55
  172.9 18.3 %all_to_all.56 = f32[64,4,512]{2,1,0:T(4,128)S(1)} all-to-all(f32[64,4,512]{2,1,0:T(4,128)S(1)} %copy.31), channel_id=1, replica_groups=mesh['wide_0'=4,'wide_1'=4,'narrow_0'=4,'narrow_1'=2] {'wide_0','wide_1'..., dimensions={0} | all-to-all | bytes 1048576 | tf_op jit(solution)/shard_map/all_to_all | solution.py:55
  192.1 4.9 all-to-all-start.5
  197.1 10.7 %all-to-all-done.5 = f32[64,4,512]{2,1,0:T(4,128)S(1)} async-done(((f32[64,4,512]{2,1,0:T(4,128)}), f32[64,4,512]{2,1,0:T(4,128)S(1)}, u32[]{:S(2)}, u32[]{:S(2)}) %all-to-all-start.5) | async-done | bytes 524320 | tf_op jit(solution)/shard_map/all_to_all | solution.py:19
  208.0 7.4 %all_to_all.57 = f32[2,64,4,512]{3,2,1,0:T(4,128)S(1)} all-to-all(f32[2,64,4,512]{3,2,1,0:T(4,128)S(1)} %broadcast_in_dim.19), channel_id=1, replica_groups=mesh['wide_0'=4,'wide_1'=4,'narrow_0'=4,'narrow_1'=2] {'narrow_1'}, dimensions={0} | all-to-all | bytes 2097152 | tf_op jit(solution)/shard_map/all_to_all | solution.py:19
  216.5 11.7 %cholesky.104 = f32[128,128]{1,0:T(8,128)S(1)} custom-call(f32[128,128]{1,0:T(8,128)S(1)} %cholesky.266), custom_call_target="Cholesky" | custom-call | tf_op jit(solution)/shard_map/jit(cholesky)/cholesky | solution.py:104
  228.4 9.8 %custom-call.31 = f32[1,128,128]{1,2,0:T(8,128)S(1)} custom-call(f32[1,128,128]{2,1,0:T(8,128)S(1)} %get-tuple-element.30), custom_call_target="InvertDiagBlocksLowerTriangular" | custom-call | tf_op jit(solution)/shard_map/jit(cholesky)/cholesky | solution.py:104
  238.9 11.7 %cholesky.217 = f32[128,128]{1,0:T(8,128)S(1)} custom-call(f32[128,128]{1,0:T(8,128)S(1)} %cholesky.270), custom_call_target="Cholesky" | custom-call | tf_op jit(solution)/shard_map/jit(cholesky)/cholesky | solution.py:104
  250.7 10.0 %custom-call.32 = f32[1,128,128]{1,2,0:T(8,128)S(1)} custom-call(f32[1,128,128]{2,1,0:T(8,128)S(1)} %get-tuple-element.27), custom_call_target="InvertDiagBlocksLowerTriangular" | custom-call | tf_op jit(solution)/shard_map/jit(cholesky)/cholesky | solution.py:104
  261.3 11.7 %cholesky.238 = f32[128,128]{1,0:T(8,128)S(1)} custom-call(f32[128,128]{1,0:T(8,128)S(1)} %cholesky.275), custom_call_target="Cholesky" | custom-call | tf_op jit(solution)/shard_map/jit(cholesky)/cholesky | solution.py:104
  273.8 9.8 %custom-call.33 = f32[1,128,128]{1,2,0:T(8,128)S(1)} custom-call(f32[1,128,128]{2,1,0:T(8,128)S(1)} %get-tuple-element.24), custom_call_target="InvertDiagBlocksLowerTriangular" | custom-call | tf_op jit(solution)/shard_map/jit(cholesky)/cholesky | solution.py:104
  284.2 11.9 %cholesky.255 = f32[128,128]{1,0:T(8,128)S(1)} custom-call(f32[128,128]{1,0:T(8,128)S(1)} %convolution_subtract_fusion.2), custom_call_target="Cholesky" | custom-call | tf_op jit(solution)/shard_map/jit(cholesky)/cholesky | solution.py:104
  300.1 8.5 %while.1 = (s32[]{:T(128)}, f32[512,512]{1,0:T(8,128)S(1)}, s32[4,2]{0,1:T(2,128)S(1)}, f32[4,128,128]{2,1,0:T(8,128)S(1)}, s32[]{:T(128)}) while((s32[]{:T(128)}, f32[512,512]{1,0:T(8,128)S(1)}, s32[4,2]{0,1:T(2,128)S(1)}, f32[4,128,128]{2,1,0:T(8,128)S(1)}, s32[]{:T(128)}) %tuple.31), condition=%wide.while_cond, body=%wide.while_body.sunk | while | flops 2 | bytes 131181 | solution.py:105
  300.8 1.4 bitcast_dynamic-update-slice_fusion.2
  308.6 39.3 %custom-call.34 = f32[4,128,128]{1,2,0:T(8,128)S(1)} custom-call(f32[4,128,128]{2,1,0:T(8,128)S(1)} %get-tuple-element.10), custom_call_target="InvertDiagBlocksLowerTriangular" | custom-call | tf_op jit(solution)/shard_map/jit(_solve_triangular)/triangular_solve | solution.py:105
  349.7 17.9 %all_to_all.58 = f32[8,64,512]{2,1,0:T(8,128)S(1)} all-to-all(f32[8,64,512]{2,1,0:T(8,128)S(1)} %broadcast_in_dim.20), channel_id=1, replica_groups=mesh['wide_0'=4,'wide_1'=4,'narrow_0'=4,'narrow_1'=2] {'narrow_0','narro..., dimensions={0} | all-to-all | bytes 2097152 | tf_op jit(solution)/shard_map/all_to_all | solution.py:19
  367.6 8.4 %fusion.34 = f32[2048,512]{1,0:T(8,128)} fusion(f32[512,2048]{1,0:T(8,128)S(1)} %copy-done.1, f32[512,512]{1,0:T(8,128)S(1)} %bitcast.75), kind=kOutput, calls=%fused_computation.77 | convolution fusion | flops 6442450944 | bytes 9437184 | tf_op jit(solution)/shard_map/dot_general | solution.py:108
  376.0 43.0 %reduce-scatter.3.cloned.1.call-done = f32[512,512]{1,0:T(8,128)} async-done(((f32[2048,512]{1,0:T(8,128)}), f32[512,512]{1,0:T(8,128)}) %reduce-scatter.3.cloned.1.call-update) | async-done | bytes 1048592 | tf_op jit(solution)/shard_map/reduce_scatter | solution.py:71
  419.1 24.2 %reduce-scatter.5.cloned.1.call-done = f32[128,512]{1,0:T(8,128)} async-done(((f32[512,512]{1,0:T(8,128)}), f32[128,512]{1,0:T(8,128)}) %reduce-scatter.5.cloned.1.call-update) | async-done | bytes 262160 | tf_op jit(solution)/shard_map/reduce_scatter | solution.py:71
  444.3 5.8 %all_to_all.59 = f32[2,1,512]{2,1,0:T(1,128)S(1)} all-to-all(f32[2,1,512]{2,1,0:T(1,128)S(1)} %broadcast_in_dim.21), channel_id=1, replica_groups=mesh['wide_0'=4,'wide_1'=4,'narrow_0'=4,'narrow_1'=2] {'narrow_1'}, dimensions={0} | all-to-all | bytes 8192 | tf_op jit(solution)/shard_map/all_to_all | solution.py:19
  450.2 17.3 %all_to_all.60 = f32[64,1,512]{2,1,0:T(1,128)S(1)} all-to-all(f32[64,1,512]{2,1,0:T(1,128)S(1)} %broadcast_in_dim.22), channel_id=1, replica_groups=mesh['wide_0'=4,'wide_1'=4,'narrow_0'=4,'narrow_1'=2] {'wide_0','wide_1'..., dimensions={0} | all-to-all | bytes 262144 | tf_op jit(solution)/shard_map/all_to_all | solution.py:19
  467.6 31.0 %all-gather.5.cloned.1.call-done = f32[2048,512]{1,0:T(8,128)} async-done(((f32[128,512]{1,0:T(8,128)}), f32[2048,512]{1,0:T(8,128)}) %all-gather.5.cloned.1.call-update) | async-done | bytes 4194320 | tf_op jit(solution)/shard_map/all_gather | solution.py:120
  498.6 2.7 broadcast_divide_fusion
  501.4 8.1 %multiply_convert_fusion = bf16[512,2048]{1,0:T(8,128)(2,1)} fusion(f32[512,512]{1,0:T(8,128)S(1)} %bitcast.76, f32[2048,512]{1,0:T(8,128)S(1)} %broadcast_divide_fusion), kind=kOutput, calls=%fused_computation.2 | convolution fusion | flops 6444548096 | bytes 7340032 | tf_op jit(solution)/shard_map/dot_general | solution.py:131
  509.5 8.5 %multiply_subtract_fusion = f32[512,2048]{1,0:T(8,128)} fusion(f32[512,2048]{1,0:T(8,128)S(1)} %copy-done.2, f32[512,512]{1,0:T(8,128)S(1)} %bitcast.77, f32[2048,512]{1,0:T(8,128)S(1)} %copy-done.3), kind=kOutput, calls=%fused_computation.3 | convolution fusion | flops 6444548096 | bytes 13631488 | tf_op jit(solution)/shard_map/dot_general | solution.py:121
  (81 shorter events, 20.5 us)
Async XLA Ops:
  7.2 117.7 %all-gather.3.cloned.1.call-start = ((), (), s32[]{:S(2)}) async-start(), calls=%async_computation.12 | async-start | bytes 17825792 | tf_op jit(solution)/shard_map/all_gather | solution.py:90
  124.8 14.4 %copy-start.4 = (f32[2048,512]{1,0:T(8,128)S(1)}, f32[2048,512]{1,0:T(8,128)}, u32[]{:S(2)}) copy-start(f32[2048,512]{1,0:T(8,128)} %param.7) | copy-start | bytes 12582916
  139.2 6.9 %copy-start = (f32[512,2048]{1,0:T(8,128)}, f32[512,2048]{1,0:T(8,128)S(1)}, u32[]{:S(2)}) copy-start(f32[512,2048]{1,0:T(8,128)S(1)} %convolution_add_fusion) | copy-start | bytes 12582916
  192.1 15.8 %all-to-all-start.5 = ((f32[64,4,512]{2,1,0:T(4,128)}), f32[64,4,512]{2,1,0:T(4,128)S(1)}, u32[]{:S(2)}, u32[]{:S(2)}) async-start(f32[64,4,512]{2,1,0:T(4,128)} %broadcast_in_dim.18), calls=%async_computation.5 | async-start | bytes 1048576 | tf_op jit(solution)/shard_map/all_to_all | solution.py:19
  197.0 222.0 %reduce-scatter.3.cloned.1.call-start = ((), (), s32[]{:S(2)}) async-start(), calls=%async_computation.13 | async-start | bytes 5242880 | tf_op jit(solution)/shard_map/reduce_scatter | solution.py:71
  347.9 19.7 %copy-start.1 = (f32[512,2048]{1,0:T(8,128)S(1)}, f32[512,2048]{1,0:T(8,128)}, u32[]{:S(2)}) copy-start(f32[512,2048]{1,0:T(8,128)} %copy-done) | copy-start | bytes 12582916
  376.0 67.3 %reduce-scatter.5.cloned.1.call-start = ((), (), s32[]{:S(2)}) async-start(), calls=%async_computation.14 | async-start | bytes 1310720 | tf_op jit(solution)/shard_map/reduce_scatter | solution.py:71
  419.1 79.6 %all-gather.5.cloned.1.call-start = ((), (), s32[]{:S(2)}) async-start(), calls=%async_computation.15 | async-start | bytes 4456448 | tf_op jit(solution)/shard_map/all_gather | solution.py:120
  501.4 8.2 %copy-start.5 = (f32[2048,512]{1,0:T(8,128)}, f32[2048,512]{1,0:T(8,128)S(1)}, u32[]{:S(2)}) copy-start(f32[2048,512]{1,0:T(8,128)S(1)} %broadcast_divide_fusion) | copy-start | bytes 12582916
  501.4 8.2 %copy-start.2 = (f32[512,2048]{1,0:T(8,128)S(1)}, f32[512,2048]{1,0:T(8,128)}, u32[]{:S(2)}) copy-start(f32[512,2048]{1,0:T(8,128)} %copy-done) | copy-start | bytes 12582916
  501.4 8.2 %copy-start.3 = (f32[2048,512]{1,0:T(8,128)S(1)}, f32[2048,512]{1,0:T(8,128)}, u32[]{:S(2)}) copy-start(f32[2048,512]{1,0:T(8,128)} %all-gather.5.cloned.1.call-done) | copy-start | bytes 12582916
Sparse Core Ops, SparseCore 0:
  10.1 114.6 all-gather.2
  376.1 42.8 reduce-scatter.2
  421.6 21.6 reduce-scatter.4
  445.3 53.2 all-gather.4
where the time goes:
time: 536 us; the launch traced here: 525 us
  waiting for transfers between devices  184 us (34%)
  blocking collectives  131 us (24%)
  other arithmetic  123 us (23%)
  matrix products  50.7 us (9%)
  between operations  17.1 us (3%)
  local copies, waits for them, and re-layouts  15.1 us (3%)
    all_to_all x6, blocking collectives, sent_to_all(): lax.all_to_all(jnp.broadcast_to(array[None], (devices, *array.shape)), ax...  87.2 us
    another operation x14, other arithmetic, body(): lower_factor = jnp.linalg.cholesky(gram_matrix)  78.8 us
    all_gather x1, waiting for transfers between devices, body(): lax.all_gather(activations, WIDE, axis=0, tiled=True)  74 us
    reduce_scatter x2, waiting for transfers between devices, own_rows(): total = lax.psum_scatter(total, axis, scatter_dimension=0, tiled=True)  67.2 us
    another operation x3, other arithmetic, body(): jax.scipy.linalg.solve_triangular(lower_factor, left_share.T, lower=True)  39.4 us
    all_gather x1, waiting for transfers between devices, body(): right_raw = lax.all_gather(right_share, WIDE, axis=0, tiled=True)  31 us
    all_to_all x2, blocking collectives, summed_on_arrival(): lax.all_to_all(tiles, axis, split_axis=0, concat_axis=0, tiled=True)  25.1 us
    all_to_all x1, blocking collectives, summed_rows(): return jnp.sum(lax.all_to_all(own, far, 0, 0, tiled=True), axis=0)  18.3 us
  transfers between devices with their start and end apart: 5, of which 5 were waited for; matrix products, arithmetic and copies ran while one was open for 1% of the time, Pallas kernels for 0%

commit v1 on v0

--- a/solution.py
+++ b/solution.py
@@ -12,6 +12,11 @@
 WIDE = ("wide_0", "wide_1")
 FEEDBACK = 0.05
 EPSILON = 1e-06
+
+
+def exchange_gather(x, axis, dim):
+    sent = jnp.stack([x] * lax.axis_size(axis))
+    return jnp.concatenate(lax.all_to_all(sent, axis, 0, 0), axis=dim)
 
 
 def sent_to_all(array, axis):
@@ -117,7 +122,7 @@
     col_squares = over_axes(
         jnp.sum(right_share * right_share, axis=0), (("wide_0", "wide_1", "narrow_0"), "narrow_1")
     )
-    right_raw = lax.all_gather(right_share, WIDE, axis=0, tiled=True)
+    right_raw = exchange_gather(right_share, WIDE, 0)
     feedback = lax.dot_general(
         ortho_left,
         right_raw,

time: 536 us -> 575 us (1.073)
  the two profiles are of different devices: /device:TPU:1 before, /device:TPU:116 now
where the time goes in v1:
time: 575 us; the launch traced here: 564 us
  waiting for transfers between devices  212 us (37%)
  other arithmetic  128 us (22%)
  blocking collectives  118 us (21%)
  matrix products  52.3 us (9%)
  starting transfers between devices  18.7 us (3%)
  local copies, waits for them, and re-layouts  18.6 us (3%)
  between operations  17.1 us (3%)
    another operation x14, other arithmetic, body(): lower_factor = jnp.linalg.cholesky(gram_matrix)  78.8 us
    all_to_all x6, blocking collectives, sent_to_all(): lax.all_to_all(jnp.broadcast_to(array[None], (devices, *array.shape)), ax...  76.7 us
    all_gather x1, waiting for transfers between devices, body(): lax.all_gather(activations, WIDE, axis=0, tiled=True)  73.7 us
    reduce_scatter x2, waiting for transfers between devices, own_rows(): total = lax.psum_scatter(total, axis, scatter_dimension=0, tiled=True)  72.5 us
    all_to_all x1, waiting for transfers between devices, exchange_gather(): return jnp.concatenate(lax.all_to_all(sent, axis, 0, 0), axis=dim)  58.4 us
    another operation x3, other arithmetic, body(): jax.scipy.linalg.solve_triangular(lower_factor, left_share.T, lower=True)  39.4 us
    all_to_all x2, blocking collectives, summed_on_arrival(): lax.all_to_all(tiles, axis, split_axis=0, concat_axis=0, tiled=True)  22.1 us
    all_to_all x1, blocking collectives, summed_rows(): return jnp.sum(lax.all_to_all(own, far, 0, 0, tiled=True), axis=0)  19.1 us
  transfers between devices with their start and end apart: 5, of which 5 were waited for; matrix products, arithmetic and copies ran while one was open for 1% of the time, Pallas kernels for 0%

profile of v1, /device:TPU:116, one launch (start us, length us, event | category | flops | bytes accessed | tf_op | source)
XLA Modules:
  0.0 564.2 jit_solution(1806415406722532986)
XLA Ops:
  9.1 28.2 %all_to_all.57 = bf16[4,512,512]{2,1,0:T(8,128)(2,1)S(1)} all-to-all(bf16[4,512,512]{2,1,0:T(8,128)(2,1)S(1)} %broadcast_in_dim.15), channel_id=1, replica_groups=mesh['wide_0'=4,'wide_1'=4,'narrow_0'=4,'narrow_1'=2] {'narrow_0'}, dimensions={0} | all-to-all | bytes 4194304 | tf_op jit(solution)/shard_map/all_to_all | solution.py:24
  37.7 7.1 %all_to_all.58 = bf16[2,4,512,512]{3,2,1,0:T(8,128)(2,1)S(1)} all-to-all(bf16[2,4,512,512]{3,2,1,0:T(8,128)(2,1)S(1)} %broadcast_in_dim.16), channel_id=1, replica_groups=mesh['wide_0'=4,'wide_1'=4,'narrow_0'=4,'narrow_1'=2] {'narrow_1'}, dimensions={0} | all-to-all | bytes 8388608 | tf_op jit(solution)/shard_map/all_to_all | solution.py:24
  47.3 73.7 %all-gather.2.cloned.1.call-done = bf16[4096,2048]{1,0:T(8,128)(2,1)} async-done(((bf16[256,2048]{1,0:T(8,128)(2,1)}), bf16[4096,2048]{1,0:T(8,128)(2,1)}) %all-gather.2.cloned.1.call-update) | async-done | bytes 16777232 | tf_op jit(solution)/shard_map/all_gather | solution.py:95
  120.9 14.4 %convolution_add_fusion = f32[512,2048]{1,0:T(8,128)S(1)} fusion(f32[512,2048]{1,0:T(8,128)} %param.6, bf16[4096,512]{1,0:T(8,128)(2,1)} %bitcast.83, bf16[4096,2048]{1,0:T(8,128)(2,1)} %all-gather.2.cloned.1.call-done), kind=kOutput, calls=%fused_computation.4 | convolution fusion | flops 8590983168 | bytes 29360128 | tf_op jit(solution)/shard_map/dot_general | solution.py:93
  135.3 6.9 %fusion.33 = f32[512,512]{1,0:T(8,128)S(1)} fusion(f32[512,2048]{1,0:T(8,128)S(1)} %convolution_add_fusion, f32[2048,512]{1,0:T(8,128)S(1)} %copy-done.3), kind=kOutput, calls=%fused_computation.77 | convolution fusion | flops 6442450944 | bytes 9437184 | tf_op jit(solution)/shard_map/dot_general | solution.py:101
  142.2 17.5 %all_to_all.59 = f32[8,64,512]{2,1,0:T(8,128)S(1)} all-to-all(f32[8,64,512]{2,1,0:T(8,128)S(1)} %bitcast.81), channel_id=1, replica_groups=mesh['wide_0'=4,'wide_1'=4,'narrow_0'=4,'narrow_1'=2] {'narrow_0','narro..., dimensions={0} | all-to-all | bytes 2097152 | tf_op jit(solution)/shard_map/all_to_all | solution.py:48
  160.9 4.6 all_to_all.60
  166.0 19.1 %all_to_all.61 = f32[64,4,512]{2,1,0:T(4,128)S(1)} all-to-all(f32[64,4,512]{2,1,0:T(4,128)S(1)} %copy.31), channel_id=1, replica_groups=mesh['wide_0'=4,'wide_1'=4,'narrow_0'=4,'narrow_1'=2] {'wide_0','wide_1'..., dimensions={0} | all-to-all | bytes 1048576 | tf_op jit(solution)/shard_map/all_to_all | solution.py:60
  186.0 10.2 %all-to-all-start.5 = ((f32[64,4,512]{2,1,0:T(4,128)}), f32[64,4,512]{2,1,0:T(4,128)S(1)}, u32[]{:S(2)}, u32[]{:S(2)}) async-start(f32[64,4,512]{2,1,0:T(4,128)} %broadcast_in_dim.18), calls=%async_computation.5 | async-start | bytes 1048576 | tf_op jit(solution)/shard_map/all_to_all | solution.py:24
  196.3 6.6 %all-to-all-done.5 = f32[64,4,512]{2,1,0:T(4,128)S(1)} async-done(((f32[64,4,512]{2,1,0:T(4,128)}), f32[64,4,512]{2,1,0:T(4,128)S(1)}, u32[]{:S(2)}, u32[]{:S(2)}) %all-to-all-start.5) | async-done | bytes 524320 | tf_op jit(solution)/shard_map/all_to_all | solution.py:24
  203.1 4.6 all_to_all.62
  208.8 11.7 %cholesky.104 = f32[128,128]{1,0:T(8,128)S(1)} custom-call(f32[128,128]{1,0:T(8,128)S(1)} %cholesky.266), custom_call_target="Cholesky" | custom-call | tf_op jit(solution)/shard_map/jit(cholesky)/cholesky | solution.py:109
  220.6 9.8 %custom-call.31 = f32[1,128,128]{1,2,0:T(8,128)S(1)} custom-call(f32[1,128,128]{2,1,0:T(8,128)S(1)} %get-tuple-element.30), custom_call_target="InvertDiagBlocksLowerTriangular" | custom-call | tf_op jit(solution)/shard_map/jit(cholesky)/cholesky | solution.py:109
  231.1 11.7 %cholesky.217 = f32[128,128]{1,0:T(8,128)S(1)} custom-call(f32[128,128]{1,0:T(8,128)S(1)} %cholesky.270), custom_call_target="Cholesky" | custom-call | tf_op jit(solution)/shard_map/jit(cholesky)/cholesky | solution.py:109
  242.9 10.0 %custom-call.32 = f32[1,128,128]{1,2,0:T(8,128)S(1)} custom-call(f32[1,128,128]{2,1,0:T(8,128)S(1)} %get-tuple-element.27), custom_call_target="InvertDiagBlocksLowerTriangular" | custom-call | tf_op jit(solution)/shard_map/jit(cholesky)/cholesky | solution.py:109
  253.5 11.7 %cholesky.238 = f32[128,128]{1,0:T(8,128)S(1)} custom-call(f32[128,128]{1,0:T(8,128)S(1)} %cholesky.275), custom_call_target="Cholesky" | custom-call | tf_op jit(solution)/shard_map/jit(cholesky)/cholesky | solution.py:109
  266.0 9.8 %custom-call.33 = f32[1,128,128]{1,2,0:T(8,128)S(1)} custom-call(f32[1,128,128]{2,1,0:T(8,128)S(1)} %get-tuple-element.24), custom_call_target="InvertDiagBlocksLowerTriangular" | custom-call | tf_op jit(solution)/shard_map/jit(cholesky)/cholesky | solution.py:109
  276.4 11.9 %cholesky.255 = f32[128,128]{1,0:T(8,128)S(1)} custom-call(f32[128,128]{1,0:T(8,128)S(1)} %convolution_subtract_fusion.2), custom_call_target="Cholesky" | custom-call | tf_op jit(solution)/shard_map/jit(cholesky)/cholesky | solution.py:109
  292.3 8.5 %while.1 = (s32[]{:T(128)}, f32[512,512]{1,0:T(8,128)S(1)}, s32[4,2]{0,1:T(2,128)S(1)}, f32[4,128,128]{2,1,0:T(8,128)S(1)}, s32[]{:T(128)}) while((s32[]{:T(128)}, f32[512,512]{1,0:T(8,128)S(1)}, s32[4,2]{0,1:T(2,128)S(1)}, f32[4,128,128]{2,1,0:T(8,128)S(1)}, s32[]{:T(128)}) %tuple.31), condition=%wide.while_cond, body=%wide.while_body.sunk | while | flops 2 | bytes 131181 | solution.py:110
  300.8 39.3 %custom-call.34 = f32[4,128,128]{1,2,0:T(8,128)S(1)} custom-call(f32[4,128,128]{2,1,0:T(8,128)S(1)} %get-tuple-element.10), custom_call_target="InvertDiagBlocksLowerTriangular" | custom-call | tf_op jit(solution)/shard_map/jit(_solve_triangular)/triangular_solve | solution.py:110
  342.0 17.5 %all_to_all.63 = f32[8,64,512]{2,1,0:T(8,128)S(1)} all-to-all(f32[8,64,512]{2,1,0:T(8,128)S(1)} %broadcast_in_dim.20), channel_id=1, replica_groups=mesh['wide_0'=4,'wide_1'=4,'narrow_0'=4,'narrow_1'=2] {'narrow_0','narro..., dimensions={0} | all-to-all | bytes 2097152 | tf_op jit(solution)/shard_map/all_to_all | solution.py:24
  359.5 8.4 %fusion.34 = f32[2048,512]{1,0:T(8,128)} fusion(f32[512,2048]{1,0:T(8,128)S(1)} %copy-done.1, f32[512,512]{1,0:T(8,128)S(1)} %bitcast.78), kind=kOutput, calls=%fused_computation.78 | convolution fusion | flops 6442450944 | bytes 9437184 | tf_op jit(solution)/shard_map/dot_general | solution.py:113
  367.9 47.4 %reduce-scatter.3.cloned.1.call-done = f32[512,512]{1,0:T(8,128)} async-done(((f32[2048,512]{1,0:T(8,128)}), f32[512,512]{1,0:T(8,128)}) %reduce-scatter.3.cloned.1.call-update) | async-done | bytes 1048592 | tf_op jit(solution)/shard_map/reduce_scatter | solution.py:76
  415.3 25.1 %reduce-scatter.5.cloned.1.call-done = f32[128,512]{1,0:T(8,128)} async-done(((f32[512,512]{1,0:T(8,128)}), f32[128,512]{1,0:T(8,128)}) %reduce-scatter.5.cloned.1.call-update) | async-done | bytes 262160 | tf_op jit(solution)/shard_map/reduce_scatter | solution.py:76
  441.4 3.7 all_to_all.64
  445.2 15.6 %all_to_all.65 = f32[64,1,512]{2,1,0:T(1,128)S(1)} all-to-all(f32[64,1,512]{2,1,0:T(1,128)S(1)} %broadcast_in_dim.22), channel_id=1, replica_groups=mesh['wide_0'=4,'wide_1'=4,'narrow_0'=4,'narrow_1'=2] {'wide_0','wide_1'..., dimensions={0} | all-to-all | bytes 262144 | tf_op jit(solution)/shard_map/all_to_all | solution.py:24
  460.8 3.5 stack.2
  464.3 8.4 %all-to-all-start.8 = ((f32[16,128,512]{2,1,0:T(8,128)}), f32[16,128,512]{2,1,0:T(8,128)}, u32[]{:S(2)}, u32[]{:S(2)}) async-start(f32[16,128,512]{2,1,0:T(8,128)} %stack.2), calls=%async_computation.10 | async-start | bytes 8388608 | tf_op jit(solution)/shard_map/all_to_all | solution.py:19
  472.8 58.4 %all-to-all-done.8 = f32[16,128,512]{2,1,0:T(8,128)} async-done(((f32[16,128,512]{2,1,0:T(8,128)}), f32[16,128,512]{2,1,0:T(8,128)}, u32[]{:S(2)}, u32[]{:S(2)}) %all-to-all-start.8) | async-done | bytes 4194336 | tf_op jit(solution)/shard_map/all_to_all | solution.py:19
  534.2 8.1 %multiply_convert_fusion = bf16[512,2048]{1,0:T(8,128)(2,1)} fusion(f32[512,512]{1,0:T(8,128)S(1)} %bitcast.79, f32[2048,512]{1,0:T(8,128)S(1)} %bitcast.82), kind=kOutput, calls=%fused_computation.2 | convolution fusion | flops 6444548096 | bytes 7340032 | tf_op jit(solution)/shard_map/dot_general | solution.py:136
  542.4 10.1 %multiply_subtract_fusion = f32[512,2048]{1,0:T(8,128)} fusion(f32[512,2048]{1,0:T(8,128)S(1)} %copy-done.2, f32[512,512]{1,0:T(8,128)S(1)} %bitcast.80, f32[2048,512]{1,0:T(8,128)} %bitcast.22), kind=kOutput, calls=%fused_computation.3 | convolution fusion | flops 6444548096 | bytes 13631488 | tf_op jit(solution)/shard_map/dot_general | solution.py:126
  552.4 4.7 broadcast_divide_fusion.1
  (78 shorter events, 27.4 us)
Async XLA Ops:
  7.2 113.8 %all-gather.2.cloned.1.call-start = ((), (), s32[]{:S(2)}) async-start(), calls=%async_computation.13 | async-start | bytes 17825792 | tf_op jit(solution)/shard_map/all_gather | solution.py:95
  120.9 14.4 %copy-start.3 = (f32[2048,512]{1,0:T(8,128)S(1)}, f32[2048,512]{1,0:T(8,128)}, u32[]{:S(2)}) copy-start(f32[2048,512]{1,0:T(8,128)} %param.7) | copy-start | bytes 12582916
  135.3 6.9 %copy-start = (f32[512,2048]{1,0:T(8,128)}, f32[512,2048]{1,0:T(8,128)S(1)}, u32[]{:S(2)}) copy-start(f32[512,2048]{1,0:T(8,128)S(1)} %convolution_add_fusion) | copy-start | bytes 12582916
  186.0 16.9 %all-to-all-start.5 = ((f32[64,4,512]{2,1,0:T(4,128)}), f32[64,4,512]{2,1,0:T(4,128)S(1)}, u32[]{:S(2)}, u32[]{:S(2)}) async-start(f32[64,4,512]{2,1,0:T(4,128)} %broadcast_in_dim.18), calls=%async_computation.5 | async-start | bytes 1048576 | tf_op jit(solution)/shard_map/all_to_all | solution.py:24
  196.2 219.1 %reduce-scatter.3.cloned.1.call-start = ((), (), s32[]{:S(2)}) async-start(), calls=%async_computation.14 | async-start | bytes 5242880 | tf_op jit(solution)/shard_map/reduce_scatter | solution.py:76
  340.1 19.4 %copy-start.1 = (f32[512,2048]{1,0:T(8,128)S(1)}, f32[512,2048]{1,0:T(8,128)}, u32[]{:S(2)}) copy-start(f32[512,2048]{1,0:T(8,128)} %copy-done) | copy-start | bytes 12582916
  367.9 72.5 %reduce-scatter.5.cloned.1.call-start = ((), (), s32[]{:S(2)}) async-start(), calls=%async_computation.15 | async-start | bytes 1310720 | tf_op jit(solution)/shard_map/reduce_scatter | solution.py:76
  464.3 66.9 %all-to-all-start.8 = ((f32[16,128,512]{2,1,0:T(8,128)}), f32[16,128,512]{2,1,0:T(8,128)}, u32[]{:S(2)}, u32[]{:S(2)}) async-start(f32[16,128,512]{2,1,0:T(8,128)} %stack.2), calls=%async_computation.10 | async-start | bytes 8388608 | tf_op jit(solution)/shard_map/all_to_all | solution.py:19
  534.2 8.1 %copy-start.2 = (f32[512,2048]{1,0:T(8,128)S(1)}, f32[512,2048]{1,0:T(8,128)}, u32[]{:S(2)}) copy-start(f32[512,2048]{1,0:T(8,128)} %copy-done) | copy-start | bytes 12582916
Sparse Core Ops, SparseCore 0:
  10.1 110.7 all-gather.1
  368.0 47.2 reduce-scatter.2
  417.9 22.5 reduce-scatter.4
